TPU v7x, 128 devices: a whole 4x4x4 slice. The times are simulated.
128 devices in a mesh: section: 8 (over z, y_lo), tensor: 16 (over y_hi, x, core).
Axes of the slice: x: 4, y: 4 (y_hi: 2, y_lo: 2; y = y_hi * 2 + y_lo), z: 4, core: 2. Of those that a mesh axis runs over, the one named last changes fastest.
Arguments:
- queries: bfloat16 [1024, 16384], P('section', 'tensor'), may hold values from -15 to 15
- tree_kv: bfloat16 [1024, 2, 1024], P('section'), may hold values from -6 to 6
- cache: bfloat16 [16, 8, 2, 8192, 128], P('section', None, None, 'tensor'), may hold values from -6 to 6
- cache_len: int32 [16], P('section'), may hold values from 1024 to 8192, as said below
- parents: int32 [16, 64], P('section'), may hold values from 0 to 62, as said below
- out_weight: bfloat16 [16384, 16384], P('tensor', 'section'), may hold values from -0.046875 to 0.046875
Outputs:
- projected: float32 [1024, 16384], P('tensor', 'section')
Inputs may be any that keep to these rules, and one draw needn't show every extreme that they name: `cache_len`: some request holds a full cache of 8192 positions; every request holds at least 1024. parents[r, 0] = 0 for the root; for j >= 1, parents[r, j] < j.
All inputs are finite; a program needn't handle non-finite values.
Results may differ from a plain program's by a relative error of at most 0.0055.
Values may be sent and summed in bfloat16 or wider, within the bound.
A program may use at most 128 MiB of HBM per device.

v0:
```python
import math

import jax
import jax.numpy as jnp
from jax import lax
from jax.sharding import PartitionSpec as P

NEGATIVE = -1e30


def tree_reach(parent_rows):
    tree_size = parent_rows.shape[-1]
    places = jnp.arange(tree_size)
    linked = (places[None, None, :] == parent_rows[:, :, None]) & (places[None, :, None] >= 1)
    reached = (linked | (places[:, None] == places[None, :])[None]).astype(jnp.float32)
    for doubling in range(tree_size.bit_length()):
        reached = jnp.minimum(
            jnp.einsum("rij,rjk->rik", reached, reached, precision=lax.Precision.HIGHEST), 1.0
        )
    return reached > 0.5


def shards(queries, tree_kv, cache, cache_len, parents, out_weight):
    request_count = cache.shape[0]
    kv_count = cache.shape[1]
    local_len = cache.shape[3]
    head_dim = cache.shape[4]
    tree_size = parents.shape[1]
    row_count = queries.shape[0]
    tensor_size = lax.axis_size("tensor")
    tensor_rank = lax.axis_index("tensor")
    own_heads = queries.shape[1] // head_dim
    all_heads = own_heads * tensor_size
    group = all_heads // kv_count
    scale = 1.0 / math.sqrt(head_dim)
    reached = tree_reach(parents)
    kv_index = tensor_rank * own_heads // group
    tree_pair = lax.dynamic_slice_in_dim(tree_kv, kv_index * head_dim, head_dim, 2)
    tree_pair = tree_pair.reshape(request_count, tree_size, 2, head_dim)
    tree_keys = tree_pair[:, :, 0]
    tree_values = tree_pair[:, :, 1]
    own_queries = queries.reshape(request_count, tree_size, own_heads, head_dim)
    gathered = lax.all_gather(queries, "tensor", axis=1, tiled=True)
    grouped = gathered.reshape(request_count, tree_size, kv_count, group, head_dim)
    offsets = tensor_rank * local_len + jnp.arange(local_len)

    def partial_request(items):
        block_queries, keys_values, length = items
        scores = (
            jnp.einsum(
                "tkgd,kpd->kgtp",
                block_queries,
                keys_values[:, 0],
                preferred_element_type=jnp.float32,
            )
            * scale
        )
        valid = offsets < length
        scores = jnp.where(valid, scores, NEGATIVE)
        peak = jnp.max(scores, axis=-1)
        weights = jnp.where(valid, jnp.exp(scores - peak[..., None]), 0.0)
        weight_total = jnp.sum(weights, axis=-1)
        summed = jnp.einsum(
            "kgtp,kpd->kgtd",
            weights.astype(jnp.bfloat16),
            keys_values[:, 1],
            preferred_element_type=jnp.float32,
        )
        return (summed, weight_total, peak)

    summed, weight_total, peak = lax.map(partial_request, (grouped, cache, cache_len))
    summed = jnp.transpose(summed, (1, 2, 0, 3, 4)).reshape(all_heads, row_count, head_dim)
    weight_total = jnp.transpose(weight_total, (1, 2, 0, 3)).reshape(all_heads, row_count)
    peak = jnp.transpose(peak, (1, 2, 0, 3)).reshape(all_heads, row_count)
    largest = lax.pmax(peak, "tensor")
    factor = jnp.exp(peak - largest)
    mine_sum, mine_total = (
        lax.psum_scatter(summed * factor[..., None], "tensor", scatter_dimension=0, tiled=True),
        lax.psum_scatter(weight_total * factor, "tensor", scatter_dimension=0, tiled=True),
    )
    mine_peak = lax.dynamic_slice_in_dim(largest, tensor_rank * own_heads, own_heads, 0)
    base_sum = jnp.transpose(
        mine_sum.reshape(own_heads, request_count, tree_size, head_dim), (1, 0, 2, 3)
    )
    base_total = jnp.transpose(mine_total.reshape(own_heads, request_count, tree_size), (1, 0, 2))
    base_peak = jnp.transpose(mine_peak.reshape(own_heads, request_count, tree_size), (1, 0, 2))
    tree_scores = (
        jnp.einsum("rthd,rsd->rhts", own_queries, tree_keys, preferred_element_type=jnp.float32)
        * scale
    )
    tree_scores = jnp.where(reached[:, None], tree_scores, NEGATIVE)
    overall = jnp.maximum(base_peak, jnp.max(tree_scores, axis=-1))
    carried = jnp.exp(base_peak - overall)
    tree_weights = jnp.where(reached[:, None], jnp.exp(tree_scores - overall[..., None]), 0.0)
    denominator = base_total * carried + jnp.sum(tree_weights, axis=-1)
    numerator = base_sum * carried[..., None] + jnp.einsum(
        "rhts,rsd->rhtd",
        tree_weights.astype(jnp.bfloat16),
        tree_values,
        preferred_element_type=jnp.float32,
    )
    attended = numerator / denominator[..., None]
    attended = (
        jnp.transpose(attended, (0, 2, 1, 3))
        .reshape(row_count, own_heads * head_dim)
        .astype(jnp.bfloat16)
    )
    rows_all = lax.all_gather(attended, "section", axis=0, tiled=True)
    return lax.psum_scatter(
        jnp.dot(rows_all, out_weight, preferred_element_type=jnp.float32),
        "tensor",
        scatter_dimension=0,
        tiled=True,
    )


def solution(mesh):
    in_specs = (
        P("section", "tensor"),
        P("section", None, None),
        P("section", None, None, "tensor", None),
        P("section"),
        P("section", None),
        P("tensor", "section"),
    )
    out_specs = P("tensor", "section")
    return jax.shard_map(shards, mesh=mesh, in_specs=in_specs, out_specs=out_specs, check_vma=False)
```

profile of v0, /device:TPU:1, one launch (start us, length us, event | category | flops | bytes accessed | tf_op | source)
XLA Modules:
  0.0 647.8 jit_solution(15883006006539774537)
XLA Ops:
  6.5 0.7 all-gather.3.cloned.1.call-update
  7.3 62.2 %all-gather.3.cloned.1.call-done = bf16[128,16384]{1,0:T(8,128)(2,1)} async-done(((bf16[128,1024]{1,0:T(8,128)(2,1)}), bf16[128,16384]{1,0:T(8,128)(2,1)}) %all-gather.3.cloned.1.call-update) | async-done | bytes 4194320 | tf_op jit(solution)/shard_map/all_gather | solution.py:43
  69.5 5.4 copy.50
  74.9 37.7 %while.15 = (s32[]{:T(128)}, f32[2,8,16,64,128]{4,3,0,2,1:T(8,128)}, f32[2,8,16,64]{3,2,1,0:T(8,128)S(1)}, f32[2,8,16,64]{3,2,1,0:T(8,128)S(1)}, s32[2]{0:T(128)...) while((s32[]{:T(128)}, ...), condition=%wide.region_3.4_spmd.clone, body=%wide.region_0.3_spmd.clone.sunk | while | flops 2201994240 | bytes 67537536 | solution.py:71
  74.9 0.6 dynamic_slice.33
  75.5 0.6 add_compare_fusion.2
  76.1 2.0 constant_dynamic-slice_fusion.9
  78.1 1.7 copy_bitcast_fusion.5
  79.8 3.8 bitcast_reduce_fusion.2
  83.6 5.3 bitcast_dynamic-update-slice_fusion.5
  89.0 4.7 fusion.58
  93.7 0.6 dynamic_slice.33
  94.3 0.6 add_compare_fusion.2
  94.9 2.0 constant_dynamic-slice_fusion.9
  96.9 1.7 copy_bitcast_fusion.5
  98.6 3.8 bitcast_reduce_fusion.2
  102.4 5.3 bitcast_dynamic-update-slice_fusion.5
  107.8 4.7 fusion.58
  112.6 0.8 reshape.55
  113.7 124.3 %all-reduce.4.cloned.1.call-done = f32[128,128]{1,0:T(8,128)} async-done(((f32[128,128]{1,0:T(8,128)}), f32[128,128]{1,0:T(8,128)}) %all-reduce.4.cloned.1.call-update) | async-done | bytes 65552 | tf_op jit(solution)/shard_map/pmax | solution.py:75
  238.0 1.5 fusion.38
  239.6 7.9 %broadcast_multiply_fusion = f32[128,128,128]{2,1,0:T(8,128)} fusion(f32[128,128,128]{2,1,0:T(8,128)} %bitcast.142, f32[128,128]{1,0:T(8,128)S(1)} %get-tuple-element.114), kind=kLoop, calls=%fused_computation.25 | loop fusion | flops 2097152 | bytes 16842752 | tf_op jit(solution)/shard_map/mul | solution.py:78
  247.6 0.9 copy-done.1
  251.8 0.7 constant_dynamic-slice_fusion.4
  252.7 115.3 %all-reduce.6.cloned.1.call-done = f32[128,128]{1,0:T(8,128)} async-done(((f32[128,128]{1,0:T(8,128)}), f32[128,128]{1,0:T(8,128)}) %all-reduce.6.cloned.1.call-update) | async-done | bytes 65552
  368.0 0.7 constant_dynamic-slice_fusion.2
  368.7 106.1 %reduce-scatter.3.cloned.1.call-done = f32[8,128,128]{2,1,0:T(8,128)} async-done(((f32[128,128,128]{2,1,0:T(8,128)}), f32[8,128,128]{2,1,0:T(8,128)}) %reduce-scatter.3.cloned.1.call-update) | async-done | bytes 524304 | tf_op jit(solution)/shard_map/reduce_scatter | solution.py:78
  474.8 1.5 fusion.20
  476.4 0.8 copy.68
  477.5 52.1 %all-gather.5.cloned.1.call-done = bf16[1024,1024]{1,0:T(8,128)(2,1)} async-done(((bf16[128,1024]{1,0:T(8,128)(2,1)}), bf16[1024,1024]{1,0:T(8,128)(2,1)}) %all-gather.5.cloned.1.call-update) | async-done | bytes 2097168 | tf_op jit(solution)/shard_map/all_gather | solution.py:108
  529.6 10.5 %fusion.40 = f32[1024,2048]{1,0:T(8,128)} fusion(bf16[1024,1024]{1,0:T(8,128)(2,1)} %all-gather.5.cloned.1.call-done, bf16[1024,2048]{1,0:T(8,128)(2,1)} %param.13), kind=kOutput, calls=%fused_computation.72 | convolution fusion | flops 4294967296 | bytes 14680064 | tf_op jit(solution)/shard_map/dot_general | solution.py:110
  540.1 100.8 %reduce-scatter.5.cloned.1.call-done = f32[64,2048]{1,0:T(8,128)} async-done(((f32[1024,2048]{1,0:T(8,128)}), f32[64,2048]{1,0:T(8,128)}) %reduce-scatter.5.cloned.1.call-update) | async-done | bytes 524304 | tf_op jit(solution)/shard_map/reduce_scatter | solution.py:109
  (49 shorter events, 3.9 us)
Async XLA Ops:
  6.5 242.0 %copy-start = (bf16[128,2,1024]{2,1,0:T(2,128)(2,1)S(1)}, bf16[128,2,1024]{2,1,0:T(2,128)(2,1)}, u32[]{:S(2)}) copy-start(bf16[128,2,1024]{2,1,0:T(2,128)(2,1)} %param.9) | copy-start | bytes 1572868
  6.5 68.3 %copy-start.3 = (s32[2]{0:T(128)S(1)}, s32[2]{0:T(128)}, u32[]{:S(2)}) copy-start(s32[2]{0:T(128)} %param.11) | copy-start | bytes 28
  6.5 63.0 %all-gather.3.cloned.1.call-start = ((), (), s32[]{:S(2)}) async-start(), calls=%async_computation.2 | async-start | bytes 4456448 | tf_op jit(solution)/shard_map/all_gather | solution.py:43
  7.3 230.7 %all-reduce.4.cloned.1.call-start = ((), (), s32[]{:S(2)}) async-start(), calls=%async_computation.3 | async-start | bytes 131072 | tf_op jit(solution)/shard_map/pmax | solution.py:75
  113.4 254.5 %all-reduce.6.cloned.1.call-start = ((), (), s32[]{:S(2)}) async-start(), calls=%async_computation.7 | async-start | bytes 131072
  239.5 235.2 %reduce-scatter.3.cloned.1.call-start = ((), (), s32[]{:S(2)}) async-start(), calls=%async_computation.4 | async-start | bytes 8912896 | tf_op jit(solution)/shard_map/reduce_scatter | solution.py:78
  247.5 0.9 copy-start.1
  247.5 1.1 copy-start.2
  247.5 2.7 copy-start.4
  247.5 282.0 %all-gather.5.cloned.1.call-start = ((), (), s32[]{:S(2)}) async-start(), calls=%async_computation.5 | async-start | bytes 2359296 | tf_op jit(solution)/shard_map/all_gather | solution.py:108
  477.2 163.7 %reduce-scatter.5.cloned.1.call-start = ((), (), s32[]{:S(2)}) async-start(), calls=%async_computation.6 | async-start | bytes 8912896 | tf_op jit(solution)/shard_map/reduce_scatter | solution.py:109
Sparse Core Ops, SparseCore 0:
  9.8 59.6 all-gather.2
  113.5 124.4 all-reduce.3
  240.6 127.2 all-reduce.5
  372.1 102.5 reduce-scatter.2
  477.3 52.1 all-gather.4
  540.3 100.6 reduce-scatter.4
where the time goes:
time: 649 us; the launch traced here: 648 us
  waiting for transfers between devices  561 us (86%)
  matrix products  32.1 us (5%)
  other arithmetic  20.2 us (3%)
  local copies, waits for them, and re-layouts  19.2 us (3%)
  between operations  14.3 us (2%)
    pmax x1, waiting for transfers between devices, shards(): largest = lax.pmax(peak, 'tensor')  124 us
    unnamed x7, waiting for transfers between devices  116 us
    reduce_scatter x1, waiting for transfers between devices, shards(): lax.psum_scatter(summed * factor[..., None], 'tensor', scatter_dimension=...  106 us
    reduce_scatter x1, waiting for transfers between devices, shards(): lax.psum_scatter(jnp.dot(rows_all, out_weight, preferred_element_type=jnp...  101 us
    all_gather x1, waiting for transfers between devices, shards(): gathered = lax.all_gather(queries, 'tensor', axis=1, tiled=True)  62.2 us
    all_gather x1, waiting for transfers between devices, shards(): rows_all = lax.all_gather(attended, 'section', axis=0, tiled=True)  52.1 us
  transfers between devices with their start and end apart: 6, of which 6 were waited for; matrix products, arithmetic and copies ran while one was open for 2% of the time, Pallas kernels for 0%

commit v1 on v0

v1 whole, which is shorter than its diff:
```python
import functools
import math

import jax
import jax.numpy as jnp
from jax import lax
from jax.experimental import pallas as pl
from jax.experimental.pallas import tpu as pltpu
from jax.sharding import PartitionSpec as P

MESH = pl.DeviceIdType.MESH
F32 = jnp.float32
BF16 = jnp.bfloat16
MASKED = -1e30
LOWEST = -3000.0
LOG2E = 1.4426950408889634

RING = 4
SLOTS = 8
QK, PV, AT, PR = range(4)


def kernel(
    queries, tree_pair, cache, cache_len, parents, weight, out,
    q_buf, kv_buf, w_buf, tree_buf, bias, reach, o_buf, stats, tree_o, tree_stats,
    send_o, near_o, pair_o, full_o, a_buf, proj, send_p, near_p, pair_p, full_p, done_p, cross_p,
    local_sem, core_send, core_recv, send_sem, recv_sem,
):
    reqs, kv_heads = cache.shape[0], cache.shape[1]
    local_len, hd = cache.shape[3], cache.shape[4]
    half = q_buf.shape[3]
    tree_size = 2 * half
    wide = q_buf.shape[4]
    heads = wide // hd
    rows = heads * half
    groups = rows // 128
    cols = w_buf.shape[2]
    scale = LOG2E / math.sqrt(hd)

    section, tensor = lax.axis_index("section"), lax.axis_index("tensor")
    core = tensor % 2
    chip = tensor // 2
    x, yh = chip % 4, chip // 4
    z, yl = section // 2, section % 2

    def ring_t(d):
        return (section, yh * 8 + ((x + d) % 4) * 2 + core)

    def ring_s(d):
        return (((z + d) % 4) * 2 + yl, tensor)

    pair_t = (section, (1 - yh) * 8 + x * 2 + core)
    pair_s = (z * 2 + (1 - yl), tensor)
    other = (section, chip * 2 + (1 - core))

    def chip_of(slot):
        return ((yh + slot // 4) % 2) * 4 + (x + slot) % 4

    def section_of(slot):
        return ((z + slot) % 4) * 2 + (yl + slot // 4) % 2

    barrier = pltpu.get_barrier_semaphore()
    greeted = [ring_t(d) for d in (1, 2, 3)] + [ring_s(d) for d in (1, 2, 3)] + [pair_t, pair_s, other]
    for target in greeted:
        pl.semaphore_signal(barrier, inc=1, device_id=target, device_id_type=MESH)
    pl.semaphore_wait(barrier, len(greeted))

    def to_core(src, dst, number):
        return pltpu.make_async_remote_copy(
            src_ref=src, dst_ref=dst, send_sem=core_send.at[number], recv_sem=core_recv.at[number],
            device_id=other, device_id_type=MESH,
        )

    def remote(src, dst, phase, r, number, target):
        return pltpu.make_async_remote_copy(
            src_ref=src, dst_ref=dst, send_sem=send_sem.at[phase, r, number], recv_sem=recv_sem.at[phase, r, number],
            device_id=target, device_id_type=MESH,
        )

    def rows_of(r, which):
        return pl.ds(pl.multiple_of(r * tree_size + which * half, half), half)

    q_local = [
        pltpu.make_async_copy(queries.at[rows_of(r, core)], q_buf.at[r, 0, core], local_sem.at[r]) for r in range(reqs)
    ]
    q_cross = [to_core(queries.at[rows_of(r, 1 - core)], q_buf.at[r, 0, core], r) for r in range(reqs)]
    for r in range(reqs):
        q_cross[r].start()
        q_local[r].start()
    c_local = [pltpu.make_async_copy(cache.at[r], kv_buf.at[r, core], local_sem.at[2 + r]) for r in range(reqs)]
    c_cross = [to_core(cache.at[r], kv_buf.at[r, core], 2 + r) for r in range(reqs)]
    w_local = pltpu.make_async_copy(weight, w_buf.at[core], local_sem.at[4])
    w_cross = to_core(weight, w_buf.at[core], 4)
    t_local = pltpu.make_async_copy(tree_pair, tree_buf, local_sem.at[5])
    c_cross[0].start()
    c_local[0].start()
    t_local.start()

    def gather_first(buf, phase, r, ring, pair):
        copies = [remote(buf.at[r, 0], buf.at[r, 4], phase, r, 4, pair)]
        for d in (1, 3, 2):
            copies.append(remote(buf.at[r, 0], buf.at[r, 4 - d], phase, r, 4 - d, ring(d)))
        return copies

    def gather_ring(buf, phase, r, slot, pair):
        return remote(buf.at[r, slot, 1], buf.at[r, 4 + slot, 1], phase, r, 4 + slot, pair)

    def gather_pair(buf, phase, r, ring):
        return [remote(buf.at[r, 4, 0], buf.at[r, 8 - d, 0], phase, r, 11 - d, ring(d)) for d in (1, 3, 2)]

    def gather_arrived(buf, phase, r, slot, target):
        remote(buf.at[r, 0], buf.at[r, slot], phase, r, slot, target).wait_recv()

    def gather_halves_arrived(buf, phase, r, slot, target):
        remote(buf.at[r, 0, 1], buf.at[r, slot, 1], phase, r, slot, target).wait_recv()
        remote(buf.at[r, 0, 0], buf.at[r, slot, 0], phase, r, slot + 3, target).wait_recv()

    def start(copies):
        for copy in copies:
            copy.start()

    def scatter_near(src, near, pairs, phase, r, slot, ring, pair):
        d = slot - 4
        return [
            remote(src.at[r, slot, 1], pairs.at[r, d], phase, r, slot, pair),
            remote(src.at[r, slot, 0], near.at[r, 4 - d], phase, r, 11 - d, ring(d)),
        ]

    def scatter_near_arrived(src, near, pairs, phase, r, target):
        for d in (1, 2, 3):
            remote(src.at[r, 4 + d, 1], pairs.at[r, d], phase, r, 4 + d, target).wait_recv()
            remote(src.at[r, 4 + d, 0], near.at[r, d], phase, r, 7 + d, target).wait_recv()

    def scatter_full(src, full, phase, r, ring, pair):
        copies = [remote(src.at[r, 4], full.at[r, 4], phase, r, 4, pair)]
        for d in (1, 3, 2):
            copies.append(remote(src.at[r, d], full.at[r, 4 - d], phase, r, 4 - d, ring(d)))
        return copies

    def scatter_full_arrived(src, full, phase, r, target):
        for slot in (1, 2, 3, 4):
            remote(src.at[r, slot], full.at[r, slot], phase, r, slot, target).wait_recv()

    for r in range(reqs):
        q_local[r].wait()
        q_cross[r].wait_recv()
        if r == 0:
            start(gather_first(q_buf, QK, 0, ring_t, pair_t))
            c_cross[1].start()
            c_local[1].start()
            w_cross.start()
            w_local.start()

    sub8 = lax.broadcasted_iota(jnp.int32, (8, 128), 0)
    eye = lax.broadcasted_iota(jnp.int32, (128, 128), 0) == lax.broadcasted_iota(jnp.int32, (128, 128), 1)
    eye2 = jnp.concatenate([eye.astype(F32), eye.astype(F32)], axis=1) > 0.5
    ones2 = jnp.ones((256, 128), BF16)

    def column(row):
        high = row.astype(BF16).astype(F32)
        both = jnp.concatenate([high, row - high], axis=1)
        spread = jnp.where(eye2, jnp.broadcast_to(both, (128, 256)), 0.0).astype(BF16)
        return jnp.dot(spread, ones2, preferred_element_type=F32)

    def compact(tall):
        return jnp.sum(jnp.where(eye, tall, 0.0), axis=0, keepdims=True)

    def stat_block(peak, total):
        block = jnp.zeros((8, 128), F32)
        for g in range(groups):
            block = jnp.where(sub8 == g, compact(jnp.broadcast_to(peak[g * 128 : g * 128 + 128], (128, 128))), block)
            block = jnp.where(sub8 == groups + g, compact(total[g * 128 : g * 128 + 128]), block)
        return block

    jrow = lax.broadcasted_iota(jnp.int32, (128, 128), 0)
    icol = lax.broadcasted_iota(jnp.int32, (128, 128), 1)
    eye_small = lax.broadcasted_iota(jnp.int32, (tree_size, tree_size), 0) == lax.broadcasted_iota(
        jnp.int32, (tree_size, tree_size), 1
    )
    above = []
    for r in range(reqs):
        own = parents[r : r + 1, :].astype(F32)
        spread = jnp.where(eye_small, jnp.broadcast_to(own, (tree_size, tree_size)), 0.0).astype(BF16)
        above.append(jnp.dot(spread, jnp.ones((tree_size, 128), BF16), preferred_element_type=F32) + float(r * tree_size))
    above = jnp.concatenate(above, axis=0)
    linked = (icol.astype(F32) == above) & (jrow % tree_size >= 1)
    reached = jnp.where(linked | (jrow == icol), 1.0, 0.0)
    for _ in range((tree_size - 1).bit_length()):
        small = reached.astype(BF16)
        reached = jnp.minimum(jnp.dot(small, small, preferred_element_type=F32), 1.0)
    reach[...] = reached

    for r in range(reqs):
        place = lax.broadcasted_iota(jnp.int32, (2 * local_len, 128), 0) + chip * (2 * local_len)
        lane = lax.broadcasted_iota(jnp.int32, (2 * local_len, 128), 1)
        bias[r] = jnp.where((lane == 0) & (place >= cache_len[r]), MASKED, 0.0).astype(BF16)

    def stacked(block):
        return jnp.concatenate([block[:, h * hd : h * hd + hd] for h in range(heads)], axis=0)

    t_local.wait()

    def tree_step(step, _):
        r, a = step // 2, step % 2
        q = stacked(q_buf[r, 0, a])
        mask = jnp.concatenate([reach[rows_of(r, core), :]] * heads, axis=0) > 0.5
        s = lax.dot_general(q, tree_buf[0], (((1,), (1,)), ((), ())), preferred_element_type=F32) * scale
        s = jnp.where(mask, s, MASKED)
        peak = jnp.max(s, axis=1, keepdims=True).astype(BF16).astype(F32)
        w = jnp.where(mask, jnp.exp2(s - peak), 0.0).astype(BF16)
        v = jnp.concatenate([tree_buf[1], jnp.ones((128, 128), BF16)], axis=1)
        o = jnp.dot(w, v, preferred_element_type=F32)
        tree_o[r, a] = o[:, :hd]
        tree_stats[r, a] = stat_block(peak, o[:, hd:])
        return 0

    lax.fori_loop(0, 2 * reqs, tree_step, 0)

    def merge(parts):
        top = functools.reduce(jnp.maximum, [st for _, st in parts])
        factors = [jnp.exp2(st - top) for _, st in parts]
        totals = sum(st * pltpu.roll(f, groups, axis=0) for (_, st), f in zip(parts, factors))
        return top, factors, totals

    def merged_values(parts, factors):
        pieces = []
        for g in range(groups):
            piece = None
            for (value, _), f in zip(parts, factors):
                term = value[g * 128 : g * 128 + 128] * column(f[g : g + 1])
                piece = term if piece is None else piece + term
            pieces.append(piece)
        return pieces

    def put(ref, pieces, block):
        for g, piece in enumerate(pieces):
            ref[pl.ds(g * 128, 128), :] = piece.astype(BF16)
        high = block.astype(BF16).astype(F32)
        ref[pl.ds(rows, 16), :] = jnp.concatenate([high, block - high], axis=0).astype(BF16)

    def got(ref):
        tail = ref[pl.ds(rows, 16), :].astype(F32)
        return ref[pl.ds(0, rows), :].astype(F32), tail[:8] + tail[8:]

    def merge_into(ref, parts):
        top, factors, totals = merge(parts)
        block = jnp.where(sub8 < groups, top, jnp.where(sub8 < 2 * groups, totals, 0.0))
        put(ref, merged_values(parts, factors), block)

    def attend(r, slot):
        k = chip_of(slot)
        keys = jnp.concatenate([kv_buf[r, 0, k, 0], kv_buf[r, 1, k, 0]], axis=0)
        keys = jnp.concatenate([keys, bias[r]], axis=1)
        values = jnp.concatenate([kv_buf[r, 0, k, 1], kv_buf[r, 1, k, 1]], axis=0)
        values = jnp.concatenate([values, jnp.ones(values.shape, BF16)], axis=1)
        first = jnp.where(lax.broadcasted_iota(jnp.int32, (rows, 128), 1) == 0, 1.0, 0.0).astype(BF16)
        for a in range(2):
            q = jnp.concatenate([stacked(q_buf[r, slot, a]), first], axis=1)
            s = lax.dot_general(q, keys, (((1,), (1,)), ((), ())), preferred_element_type=F32)
            peak = jnp.maximum(jnp.max(s, axis=1, keepdims=True) * scale, LOWEST).astype(BF16).astype(F32)
            w = jnp.exp2(s * scale - peak).astype(BF16)
            o = jnp.dot(w, values, preferred_element_type=F32)
            o_buf[r, slot, a] = o[:, :hd]
            stats[r, slot, a] = stat_block(peak, o[:, hd:])

    def emit_own(r, slot, a):
        value = o_buf[r, slot, a]
        put(send_o.at[r, slot, a], [value[g * 128 : g * 128 + 128] for g in range(groups)], stats[r, slot, a])

    def scatter_sums(r):
        scatter_near_arrived(send_o, near_o, pair_o, PV, r, pair_t)
        merge_into(
            send_o.at[r, 4, 0],
            [(o_buf[r, 4, 0], stats[r, 4, 0])] + [got(near_o.at[r, d]) for d in (1, 2, 3)],
        )
        emit_own(r, 4, 1)
        copies = scatter_full(send_o, full_o, PV, r, ring_t, pair_t)
        copies[0].start()

        def ring_step(d, _):
            merge_into(send_o.at[r, d, 1], [(o_buf[r, d, 1], stats[r, d, 1]), got(pair_o.at[r, d])])
            emit_own(r, d, 0)
            return 0

        lax.fori_loop(1, RING, ring_step, 0)
        start(copies[1:])

    def finish_sums(r):
        scatter_full_arrived(send_o, full_o, PV, r, pair_t)

        def half_step(a, _):
            parts = [(o_buf[r, 0, a], stats[r, 0, a]), (tree_o[r, a], tree_stats[r, a])]
            parts += [got(full_o.at[r, slot, a]) for slot in (1, 2, 3, 4)]
            top, factors, totals = merge(parts)
            inverse = 1.0 / pltpu.roll(jnp.where((sub8 >= groups) & (sub8 < 2 * groups), totals, 1.0), 8 - groups, axis=0)
            factors = [f * inverse for f in factors]
            pieces = merged_values(parts, factors)
            per = 128 // half
            for h in range(heads):
                piece = pieces[h // per][(h % per) * half : (h % per + 1) * half]
                a_buf[r, 0, a, :, h * hd : h * hd + hd] = piece.astype(BF16)
            return 0

        lax.fori_loop(0, 2, half_step, 0)
        start(gather_first(a_buf, AT, r, ring_s, pair_s))

    def pass_attended(r):
        gather_arrived(a_buf, AT, r, 4, pair_s)
        start(gather_pair(a_buf, AT, r, ring_s))
        for d in (1, 3, 2):
            gather_arrived(a_buf, AT, r, d, pair_s)
            gather_ring(a_buf, AT, r, d, pair_s).start()

    def project(r):
        for slot in (5, 6, 7):
            gather_halves_arrived(a_buf, AT, r, slot, pair_s)
        step_cols = 512
        order = [section_of(slot) for slot in range(SLOTS)]

        def tile(n, _):
            at = pl.ds(pl.multiple_of(n * step_cols, step_cols), step_cols)
            acc = None
            for a in range(2):
                left = a_buf[r, :, a].reshape(SLOTS * half, wide)
                term = jnp.dot(left, w_buf[a, :, at], preferred_element_type=F32)
                acc = term if acc is None else acc + term
            for slot in range(SLOTS):
                proj[r, order[slot], :, at] = acc[slot * half : slot * half + half]
            return 0

        lax.fori_loop(0, cols // step_cols, tile, 0)

        for slot in (5, 6, 7):
            for a in range(2):
                send_p[r, slot, a] = proj[r, chip_of(slot), :, a * (cols // 2) : (a + 1) * (cols // 2)].astype(BF16)
            start(scatter_near(send_p, near_p, pair_p, PR, r, slot, ring_t, pair_t))

    def own_proj(r, slot, a):
        return proj[r, chip_of(slot), :, a * (cols // 2) : (a + 1) * (cols // 2)]

    def scatter_projected(r):
        scatter_near_arrived(send_p, near_p, pair_p, PR, r, pair_t)
        total = own_proj(r, 4, 0)
        for d in (1, 2, 3):
            total += near_p[r, d].astype(F32)
        send_p[r, 4, 0] = total.astype(BF16)
        send_p[r, 4, 1] = own_proj(r, 4, 1).astype(BF16)
        copies = scatter_full(send_p, full_p, PR, r, ring_t, pair_t)
        copies[0].start()
        for copy, d in zip(copies[1:], (1, 3, 2)):
            send_p[r, d, 0] = own_proj(r, d, 0).astype(BF16)
            send_p[r, d, 1] = (own_proj(r, d, 1) + pair_p[r, d].astype(F32)).astype(BF16)
            copy.start()

    def finish_projected(r):
        scatter_full_arrived(send_p, full_p, PR, r, pair_t)
        for a in range(2):
            total = own_proj(r, 0, a)
            for slot in (1, 2, 3, 4):
                total += full_p[r, slot, a].astype(F32)
            done_p[r, :, a * (cols // 2) : (a + 1) * (cols // 2)] = total

    def step(i, _):
        r, slot = i // SLOTS, i % SLOTS

        for number in range(reqs):

            @pl.when(i == number * SLOTS)
            def _():
                c_local[number].wait()
                c_cross[number].wait_recv()

        @pl.when(slot == 1)
        def _():
            gather_arrived(q_buf, QK, r, 4, pair_t)
            start(gather_pair(q_buf, QK, r, ring_t))

        @pl.when((slot >= 1) & (slot <= 3))
        def _():
            gather_arrived(q_buf, QK, r, slot, pair_t)
            gather_ring(q_buf, QK, r, slot, pair_t).start()

        @pl.when(i == 1)
        def _():
            start(gather_first(q_buf, QK, 1, ring_t, pair_t))

        @pl.when(slot >= 5)
        def _():
            gather_halves_arrived(q_buf, QK, r, slot, pair_t)

        @pl.when(i == SLOTS + 3)
        def _():
            scatter_sums(0)

        attend(r, slot)

        for last in (5, 6, 7):

            @pl.when(slot == last)
            def _():
                for a in range(2):
                    emit_own(r, last, a)
                start(scatter_near(send_o, near_o, pair_o, PV, r, last, ring_t, pair_t))

        return 0

    lax.fori_loop(0, reqs * SLOTS, step, 0)

    finish_sums(0)
    scatter_sums(1)
    pass_attended(0)
    finish_sums(1)
    w_local.wait()
    w_cross.wait_recv()
    project(0)
    pass_attended(1)
    scatter_projected(0)
    project(1)
    finish_projected(0)
    scatter_projected(1)
    finish_projected(1)

    crossing = to_core(done_p.at[1 - core], cross_p, 5)
    crossing.start()
    out[pl.ds(pl.multiple_of(core * half, half), half), :] = done_p[core]
    crossing.wait_recv()
    out[pl.ds(pl.multiple_of((1 - core) * half, half), half), :] = cross_p[...]

    for r in range(reqs):
        q_cross[r].wait_send()
        c_cross[r].wait_send()
    w_cross.wait_send()
    crossing.wait_send()
    for r in range(reqs):
        for phase, buf, ring, pair in ((QK, q_buf, ring_t, pair_t), (AT, a_buf, ring_s, pair_s)):
            copies = gather_first(buf, phase, r, ring, pair) + gather_pair(buf, phase, r, ring)
            copies += [gather_ring(buf, phase, r, d, pair) for d in (1, 2, 3)]
            for copy in copies:
                copy.wait_send()
        for phase, src, near, pairs, full in (
            (PV, send_o, near_o, pair_o, full_o),
            (PR, send_p, near_p, pair_p, full_p),
        ):
            copies = scatter_full(src, full, phase, r, ring_t, pair_t)
            for slot in (5, 6, 7):
                copies += scatter_near(src, near, pairs, phase, r, slot, ring_t, pair_t)
            for copy in copies:
                copy.wait_send()


def shards(queries, tree_kv, cache, cache_len, parents, out_weight):
    reqs, kv_heads, _, local_len, hd = cache.shape
    tokens, wide = queries.shape
    half = tokens // reqs // 2
    cols = out_weight.shape[1]
    rows = wide // hd * half
    kv = lax.axis_index("tensor") // 2
    tree_pair = jnp.swapaxes(lax.dynamic_slice_in_dim(tree_kv, kv * hd, hd, 2), 0, 1)
    hbm = pl.BlockSpec(memory_space=pl.ANY)
    vmem = pl.BlockSpec(memory_space=pltpu.VMEM)
    smem = pl.BlockSpec(memory_space=pltpu.SMEM)
    return pl.pallas_call(
        kernel,
        name="verify",
        out_shape=jax.ShapeDtypeStruct((2 * half, cols), F32),
        in_specs=[hbm, hbm, hbm, smem, vmem, hbm],
        out_specs=vmem,
        scratch_shapes=[
            pltpu.VMEM((reqs, SLOTS, 2, half, wide), BF16),
            pltpu.VMEM((reqs, 2, kv_heads, 2, local_len, hd), BF16),
            pltpu.VMEM((2, wide, cols), BF16),
            pltpu.VMEM((2, tokens, hd), BF16),
            pltpu.VMEM((reqs, 2 * local_len, 128), BF16),
            pltpu.VMEM((tokens, tokens), F32),
            pltpu.VMEM((reqs, SLOTS, 2, rows, hd), F32),
            pltpu.VMEM((reqs, SLOTS, 2, 8, 128), F32),
            pltpu.VMEM((reqs, 2, rows, hd), F32),
            pltpu.VMEM((reqs, 2, 8, 128), F32),
            pltpu.VMEM((reqs, SLOTS, 2, rows + 16, hd), BF16),
            pltpu.VMEM((reqs, RING, rows + 16, hd), BF16),
            pltpu.VMEM((reqs, RING, rows + 16, hd), BF16),
            pltpu.VMEM((reqs, 5, 2, rows + 16, hd), BF16),
            pltpu.VMEM((reqs, SLOTS, 2, half, wide), BF16),
            pltpu.VMEM((reqs, SLOTS, half, cols), F32),
            pltpu.VMEM((reqs, SLOTS, 2, half, cols // 2), BF16),
            pltpu.VMEM((reqs, RING, half, cols // 2), BF16),
            pltpu.VMEM((reqs, RING, half, cols // 2), BF16),
            pltpu.VMEM((reqs, 5, 2, half, cols // 2), BF16),
            pltpu.VMEM((reqs, half, cols), F32),
            pltpu.VMEM((half, cols), F32),
            pltpu.SemaphoreType.DMA((6,)),
            pltpu.SemaphoreType.DMA((6,)),
            pltpu.SemaphoreType.DMA((6,)),
            pltpu.SemaphoreType.DMA((4, reqs, 11)),
            pltpu.SemaphoreType.DMA((4, reqs, 11)),
        ],
        compiler_params=pltpu.CompilerParams(
            collective_id=0, has_side_effects=True, vmem_limit_bytes=60 * 2**20
        ),
        cost_estimate=pl.CostEstimate(flops=2 * 2**33, bytes_accessed=10 * 2**20, transcendentals=2**23),
    )(queries, tree_pair, cache, cache_len, parents, out_weight)


def solution(mesh):
    in_specs = (
        P("section", "tensor"),
        P("section", None, None),
        P("section", None, None, "tensor", None),
        P("section"),
        P("section", None),
        P("tensor", "section"),
    )
    out_specs = P("tensor", "section")
    return jax.shard_map(shards, mesh=mesh, in_specs=in_specs, out_specs=out_specs, check_vma=False)
```

time: 649 us -> 91.1 us (0.14)
  waiting for transfers between devices: 561 us -> 0 us
  Pallas kernels: 0 us -> 87.3 us
  matrix products: 32.1 us -> 0 us
  other arithmetic: 20.2 us -> 0 us
  local copies, waits for them, and re-layouts: 19.2 us -> 3.6 us
  between operations: 14.3 us -> 0.01 us
    reduce_scatter x2 -> x0, waiting for transfers between devices: 207 us -> none  [the longest x1 106 us: shards(): lax.psum_scatter(summed * factor[..., None], 'tensor', scatter_dimension=...]
    pmax x1 -> x0, waiting for transfers between devices: 124 us -> none  [shards(): largest = lax.pmax(peak, 'tensor')]
    unnamed x7 -> x0, waiting for transfers between devices: 116 us -> none
    all_gather x2 -> x0, waiting for transfers between devices: 114 us -> none  [the longest x1 62.2 us: shards(): gathered = lax.all_gather(queries, 'tensor', axis=1, tiled=True)]
    pallas_call x0 -> x1, Pallas kernels: none -> 87.3 us  [shards(): pl.pallas_call(kernel, name='verify', out_shape=jax.ShapeDtypeStruct((2 *...]
    dot_general x14 -> x0, matrix products: 32.1 us -> none  [the longest x2 10.7 us: partial_request(): jnp.einsum('kgtp,kpd->kgtd', weights.astype(jnp.bfloat16), keys_values[:,...]
    reduce_sum x3 -> x0, other arithmetic: 9.52 us -> none  [the longest x2 9.39 us: partial_request(): weight_total = jnp.sum(weights, axis=-1)]
    mul x2 -> x0, other arithmetic: 9.42 us -> none  [the longest x1 7.9 us: shards(): summed * factor[..., None]]
  transfers between devices with their start and end apart: 6 -> 0, of which waited for: 6 -> 0; matrix products, arithmetic and copies ran while one was open for 2% -> 0% of each run, Pallas kernels for 0% -> 0%
where the time goes in v1:
time: 91.1 us; the launch traced here: 90.9 us
  Pallas kernels  87.3 us (96%)
  local copies, waits for them, and re-layouts  3.6 us (4%)
    pallas_call x1, Pallas kernels, shards(): pl.pallas_call(kernel, name='verify', out_shape=jax.ShapeDtypeStruct((2 *...  87.3 us
    unnamed x4, local copies, waits for them, and re-layouts  3.55 us

profile of v1, /device:TPU:1, one launch (start us, length us, event | category | flops | bytes accessed | tf_op | source)
XLA Modules:
  0.0 90.9 jit_solution(4480438673215647343)
XLA Ops:
  0.0 0.0 copy-start
  0.0 1.0 %copy-done = bf16[128,2,1024]{2,1,0:T(2,128)(2,1)S(1)} copy-done((bf16[128,2,1024]{2,1,0:T(2,128)(2,1)S(1)}, bf16[128,2,1024]{2,1,0:T(2,128)(2,1)}, u32[]{:S(2)}) %copy-start) | copy-done | bytes 524312
  1.1 0.6 copy.10
  1.7 87.3 %verify.1 = f32[64,2048]{1,0:T(8,128)} custom-call(bf16[128,1024]{1,0:T(8,128)(2,1)} %queries.1, bf16[2,128,128]{2,1,0:T(8,128)(2,1)} %bitcast.3, bf16[2,8,2,512,128]{4,3,2,1,0:T(8,128)(2,1)} %cache.1, s32[2]{0:T(128)} %cache_len.1, s32[2,64]{1,0:T(2,128)} %parents.1, bf16[1024,2048]{1,0:T(8,128)(2,1)} %weight.1), custom_call_target="tpu_custom_call" | custom-call | flops 17179869184 | bytes 10485760 | tf_op jit(solution)/shard_map/verify/pallas_call | solution.py:462
  89.0 1.9 %copy.12 = f32[64,2048]{1,0:T(8,128)} copy(f32[64,2048]{1,0:T(8,128)} %verify.1) | data formatting | bytes 1048576
  (1 shorter events, 0.0 us)
Async XLA Ops:
  0.0 1.0 %copy-start = (bf16[128,2,1024]{2,1,0:T(2,128)(2,1)S(1)}, bf16[128,2,1024]{2,1,0:T(2,128)(2,1)}, u32[]{:S(2)}) copy-start(bf16[128,2,1024]{2,1,0:T(2,128)(2,1)} %param.7) | copy-start | bytes 1572868

commit v2 on v1

--- a/solution.py
+++ b/solution.py
@@ -304,16 +304,16 @@
         lax.fori_loop(0, 2, half_step, 0)
         start(gather_first(a_buf, AT, r, ring_s, pair_s))
 
+    def pass_whole(r):
+        return [remote(a_buf.at[r, 4], a_buf.at[r, 8 - d], AT, r, 8 - d, ring_s(d)) for d in (1, 3, 2)]
+
     def pass_attended(r):
         gather_arrived(a_buf, AT, r, 4, pair_s)
-        start(gather_pair(a_buf, AT, r, ring_s))
-        for d in (1, 3, 2):
-            gather_arrived(a_buf, AT, r, d, pair_s)
-            gather_ring(a_buf, AT, r, d, pair_s).start()
+        start(pass_whole(r))
 
     def project(r):
-        for slot in (5, 6, 7):
-            gather_halves_arrived(a_buf, AT, r, slot, pair_s)
+        for slot in (1, 2, 3, 5, 6, 7):
+            gather_arrived(a_buf, AT, r, slot, pair_s)
         step_cols = 512
         order = [section_of(slot) for slot in range(SLOTS)]
 
@@ -432,11 +432,11 @@
     w_cross.wait_send()
     crossing.wait_send()
     for r in range(reqs):
-        for phase, buf, ring, pair in ((QK, q_buf, ring_t, pair_t), (AT, a_buf, ring_s, pair_s)):
-            copies = gather_first(buf, phase, r, ring, pair) + gather_pair(buf, phase, r, ring)
-            copies += [gather_ring(buf, phase, r, d, pair) for d in (1, 2, 3)]
-            for copy in copies:
-                copy.wait_send()
+        copies = gather_first(q_buf, QK, r, ring_t, pair_t) + gather_pair(q_buf, QK, r, ring_t)
+        copies += [gather_ring(q_buf, QK, r, d, pair_t) for d in (1, 2, 3)]
+        copies += gather_first(a_buf, AT, r, ring_s, pair_s) + pass_whole(r)
+        for copy in copies:
+            copy.wait_send()
         for phase, src, near, pairs, full in (
             (PV, send_o, near_o, pair_o, full_o),
             (PR, send_p, near_p, pair_p, full_p),

time: 91.1 us -> 88.4 us (0.970)
  Pallas kernels: 87.3 us -> 84.5 us
    pallas_call x1, Pallas kernels: 87.3 us -> 84.5 us  [shards(): pl.pallas_call(kernel, name='verify', out_shape=jax.ShapeDtypeStruct((2 *...]
where the time goes in v2:
time: 88.4 us; the launch traced here: 88.2 us
  Pallas kernels  84.5 us (96%)
  local copies, waits for them, and re-layouts  3.6 us (4%)
    pallas_call x1, Pallas kernels, shards(): pl.pallas_call(kernel, name='verify', out_shape=jax.ShapeDtypeStruct((2 *...  84.5 us
    unnamed x4, local copies, waits for them, and re-layouts  3.55 us

profile of v2, /device:TPU:1, one launch (start us, length us, event | category | flops | bytes accessed | tf_op | source)
XLA Modules:
  0.0 88.2 jit_solution(3147864837861570377)
XLA Ops:
  0.0 0.0 copy-start
  0.0 1.0 %copy-done = bf16[128,2,1024]{2,1,0:T(2,128)(2,1)S(1)} copy-done((bf16[128,2,1024]{2,1,0:T(2,128)(2,1)S(1)}, bf16[128,2,1024]{2,1,0:T(2,128)(2,1)}, u32[]{:S(2)}) %copy-start) | copy-done | bytes 524312
  1.1 0.6 copy.10
  1.7 84.5 %verify.1 = f32[64,2048]{1,0:T(8,128)} custom-call(bf16[128,1024]{1,0:T(8,128)(2,1)} %queries.1, bf16[2,128,128]{2,1,0:T(8,128)(2,1)} %bitcast.3, bf16[2,8,2,512,128]{4,3,2,1,0:T(8,128)(2,1)} %cache.1, s32[2]{0:T(128)} %cache_len.1, s32[2,64]{1,0:T(2,128)} %parents.1, bf16[1024,2048]{1,0:T(8,128)(2,1)} %weight.1), custom_call_target="tpu_custom_call" | custom-call | flops 17179869184 | bytes 10485760 | tf_op jit(solution)/shard_map/verify/pallas_call | solution.py:462
  86.3 1.9 %copy.12 = f32[64,2048]{1,0:T(8,128)} copy(f32[64,2048]{1,0:T(8,128)} %verify.1) | data formatting | bytes 1048576
  (1 shorter events, 0.0 us)
Async XLA Ops:
  0.0 1.0 %copy-start = (bf16[128,2,1024]{2,1,0:T(2,128)(2,1)S(1)}, bf16[128,2,1024]{2,1,0:T(2,128)(2,1)}, u32[]{:S(2)}) copy-start(bf16[128,2,1024]{2,1,0:T(2,128)(2,1)} %param.7) | copy-start | bytes 1572868

commit v3 on v2

--- a/solution.py
+++ b/solution.py
@@ -277,13 +277,10 @@
         copies = scatter_full(send_o, full_o, PV, r, ring_t, pair_t)
         copies[0].start()
 
-        def ring_step(d, _):
+        for copy, d in zip(copies[1:], (1, 3, 2)):
             merge_into(send_o.at[r, d, 1], [(o_buf[r, d, 1], stats[r, d, 1]), got(pair_o.at[r, d])])
             emit_own(r, d, 0)
-            return 0
-
-        lax.fori_loop(1, RING, ring_step, 0)
-        start(copies[1:])
+            copy.start()
 
     def finish_sums(r):
         scatter_full_arrived(send_o, full_o, PV, r, pair_t)
@@ -328,12 +325,12 @@
                 proj[r, order[slot], :, at] = acc[slot * half : slot * half + half]
             return 0
 
-        lax.fori_loop(0, cols // step_cols, tile, 0)
-
-        for slot in (5, 6, 7):
-            for a in range(2):
+        steps = cols // step_cols // 2
+        for a in (1, 0):
+            lax.fori_loop(a * steps, (a + 1) * steps, tile, 0)
+            for slot in (5, 7, 6):
                 send_p[r, slot, a] = proj[r, chip_of(slot), :, a * (cols // 2) : (a + 1) * (cols // 2)].astype(BF16)
-            start(scatter_near(send_p, near_p, pair_p, PR, r, slot, ring_t, pair_t))
+                scatter_near(send_p, near_p, pair_p, PR, r, slot, ring_t, pair_t)[1 - a].start()
 
     def own_proj(r, slot, a):
         return proj[r, chip_of(slot), :, a * (cols // 2) : (a + 1) * (cols // 2)]
@@ -388,7 +385,7 @@
         def _():
             gather_halves_arrived(q_buf, QK, r, slot, pair_t)
 
-        @pl.when(i == SLOTS + 3)
+        @pl.when(i == SLOTS + 2)
         def _():
             scatter_sums(0)
 
@@ -495,7 +492,7 @@
             pltpu.SemaphoreType.DMA((4, reqs, 11)),
         ],
         compiler_params=pltpu.CompilerParams(
-            collective_id=0, has_side_effects=True, vmem_limit_bytes=60 * 2**20
+            collective_id=0, has_side_effects=True, vmem_limit_bytes=50 * 2**20
         ),
         cost_estimate=pl.CostEstimate(flops=2 * 2**33, bytes_accessed=10 * 2**20, transcendentals=2**23),
     )(queries, tree_pair, cache, cache_len, parents, out_weight)

time: 88.4 us -> 85.9 us (0.972)
  Pallas kernels: 84.5 us -> 81.5 us
    pallas_call x1, Pallas kernels: 84.5 us -> 81.5 us  [shards(): pl.pallas_call(kernel, name='verify', out_shape=jax.ShapeDtypeStruct((2 *...]
    unnamed x4 -> x10, local copies, waits for them, and re-layouts: 3.55 us -> 4.13 us
where the time goes in v3:
time: 85.9 us; the launch traced here: 85.7 us
  Pallas kernels  81.5 us (95%)
  local copies, waits for them, and re-layouts  4.17 us (5%)
    pallas_call x1, Pallas kernels, shards(): pl.pallas_call(kernel, name='verify', out_shape=jax.ShapeDtypeStruct((2 *...  81.5 us
    unnamed x10, local copies, waits for them, and re-layouts  4.13 us

profile of v3, /device:TPU:1, one launch (start us, length us, event | category | flops | bytes accessed | tf_op | source)
XLA Modules:
  0.0 85.7 jit_solution(11168321870791286919)
XLA Ops:
  0.0 0.0 copy-start
  0.0 1.0 %copy-done = bf16[128,2,1024]{2,1,0:T(2,128)(2,1)S(1)} copy-done((bf16[128,2,1024]{2,1,0:T(2,128)(2,1)S(1)}, bf16[128,2,1024]{2,1,0:T(2,128)(2,1)}, u32[]{:S(2)}) %copy-start) | copy-done | bytes 524312
  1.1 0.0 copy-start.1
  1.1 0.9 %copy-done.1 = bf16[128,1024]{1,0:T(8,128)(2,1)S(1)} copy-done((bf16[128,1024]{1,0:T(8,128)(2,1)S(1)}, bf16[128,1024]{1,0:T(8,128)(2,1)}, u32[]{:S(2)}) %copy-start.1) | copy-done | bytes 262168
  2.1 0.0 copy-start.2
  2.1 0.7 copy-done.2
  2.7 0.0 copy-start.3
  2.7 0.7 copy-done.3
  3.4 81.5 %verify.1 = f32[64,2048]{1,0:T(8,128)S(1)} custom-call(bf16[128,1024]{1,0:T(8,128)(2,1)S(1)} %copy-done.1, bf16[2,128,128]{2,1,0:T(8,128)(2,1)S(1)} %bitcast.3, bf16[2,8,2,512,128]{4,3,2,1,0:T(8,128)(2,1)} %cache.1, s32[2]{0:T(128)S(1)} %copy-done.3, s32[2,64]{1,0:T(2,128)S(1)} %copy-done.2, bf16[1024,2048]{1,0:T(8,128)(2,1)} %weight.1), custom_call_target="tpu_custom_call" | custom-call | flops 17179869184 | bytes 10485760 | tf_op jit(solution)/shard_map/verify/pallas_call | solution.py:459
  84.9 0.8 copy.12
  (2 shorter events, 0.1 us)
Async XLA Ops:
  0.0 1.0 %copy-start = (bf16[128,2,1024]{2,1,0:T(2,128)(2,1)S(1)}, bf16[128,2,1024]{2,1,0:T(2,128)(2,1)}, u32[]{:S(2)}) copy-start(bf16[128,2,1024]{2,1,0:T(2,128)(2,1)} %param.7) | copy-start | bytes 1572868
  1.1 1.0 %copy-start.1 = (bf16[128,1024]{1,0:T(8,128)(2,1)S(1)}, bf16[128,1024]{1,0:T(8,128)(2,1)}, u32[]{:S(2)}) copy-start(bf16[128,1024]{1,0:T(8,128)(2,1)} %queries.1) | copy-start | bytes 786436
  2.1 0.7 copy-start.2
  2.7 0.7 copy-start.3

commit v4 on v3

--- a/solution.py
+++ b/solution.py
@@ -63,7 +63,6 @@
     greeted = [ring_t(d) for d in (1, 2, 3)] + [ring_s(d) for d in (1, 2, 3)] + [pair_t, pair_s, other]
     for target in greeted:
         pl.semaphore_signal(barrier, inc=1, device_id=target, device_id_type=MESH)
-    pl.semaphore_wait(barrier, len(greeted))
 
     def to_core(src, dst, number):
         return pltpu.make_async_remote_copy(
@@ -85,8 +84,10 @@
     ]
     q_cross = [to_core(queries.at[rows_of(r, 1 - core)], q_buf.at[r, 0, core], r) for r in range(reqs)]
     for r in range(reqs):
+        q_local[r].start()
+    pl.semaphore_wait(barrier, len(greeted))
+    for r in range(reqs):
         q_cross[r].start()
-        q_local[r].start()
     c_local = [pltpu.make_async_copy(cache.at[r], kv_buf.at[r, core], local_sem.at[2 + r]) for r in range(reqs)]
     c_cross = [to_core(cache.at[r], kv_buf.at[r, core], 2 + r) for r in range(reqs)]
     w_local = pltpu.make_async_copy(weight, w_buf.at[core], local_sem.at[4])
@@ -413,8 +414,8 @@
     pass_attended(1)
     scatter_projected(0)
     project(1)
+    scatter_projected(1)
     finish_projected(0)
-    scatter_projected(1)
     finish_projected(1)
 
     crossing = to_core(done_p.at[1 - core], cross_p, 5)

time: 85.9 us -> 86 us (level)
  no operation moved by 1% of the time
where the time goes in v4:
time: 86 us; the launch traced here: 85.8 us
  Pallas kernels  81.6 us (95%)
  local copies, waits for them, and re-layouts  4.17 us (5%)
    pallas_call x1, Pallas kernels, shards(): pl.pallas_call(kernel, name='verify', out_shape=jax.ShapeDtypeStruct((2 *...  81.6 us
    unnamed x10, local copies, waits for them, and re-layouts  4.13 us

profile of v4, /device:TPU:1, one launch (start us, length us, event | category | flops | bytes accessed | tf_op | source)
XLA Modules:
  0.0 85.8 jit_solution(15856278467534650204)
XLA Ops:
  0.0 0.0 copy-start
  0.0 1.0 %copy-done = bf16[128,2,1024]{2,1,0:T(2,128)(2,1)S(1)} copy-done((bf16[128,2,1024]{2,1,0:T(2,128)(2,1)S(1)}, bf16[128,2,1024]{2,1,0:T(2,128)(2,1)}, u32[]{:S(2)}) %copy-start) | copy-done | bytes 524312
  1.1 0.0 copy-start.1
  1.1 0.9 %copy-done.1 = bf16[128,1024]{1,0:T(8,128)(2,1)S(1)} copy-done((bf16[128,1024]{1,0:T(8,128)(2,1)S(1)}, bf16[128,1024]{1,0:T(8,128)(2,1)}, u32[]{:S(2)}) %copy-start.1) | copy-done | bytes 262168
  2.1 0.0 copy-start.2
  2.1 0.7 copy-done.2
  2.7 0.0 copy-start.3
  2.7 0.7 copy-done.3
  3.4 81.6 %verify.1 = f32[64,2048]{1,0:T(8,128)S(1)} custom-call(bf16[128,1024]{1,0:T(8,128)(2,1)S(1)} %copy-done.1, bf16[2,128,128]{2,1,0:T(8,128)(2,1)S(1)} %bitcast.3, bf16[2,8,2,512,128]{4,3,2,1,0:T(8,128)(2,1)} %cache.1, s32[2]{0:T(128)S(1)} %copy-done.3, s32[2,64]{1,0:T(2,128)S(1)} %copy-done.2, bf16[1024,2048]{1,0:T(8,128)(2,1)} %weight.1), custom_call_target="tpu_custom_call" | custom-call | flops 17179869184 | bytes 10485760 | tf_op jit(solution)/shard_map/verify/pallas_call | solution.py:460
  85.0 0.8 copy.12
  (2 shorter events, 0.1 us)
Async XLA Ops:
  0.0 1.0 %copy-start = (bf16[128,2,1024]{2,1,0:T(2,128)(2,1)S(1)}, bf16[128,2,1024]{2,1,0:T(2,128)(2,1)}, u32[]{:S(2)}) copy-start(bf16[128,2,1024]{2,1,0:T(2,128)(2,1)} %param.7) | copy-start | bytes 1572868
  1.1 1.0 %copy-start.1 = (bf16[128,1024]{1,0:T(8,128)(2,1)S(1)}, bf16[128,1024]{1,0:T(8,128)(2,1)}, u32[]{:S(2)}) copy-start(bf16[128,1024]{1,0:T(8,128)(2,1)} %queries.1) | copy-start | bytes 786436
  2.1 0.7 copy-start.2
  2.7 0.7 copy-start.3
